TPU v7x, 32 devices: a whole 2x2x4 slice. The times are simulated.
32 devices in a mesh: inst: 16 (over z, x, core), tp: 2 (over y).
Axes of the slice: x: 2, y: 2, z: 4, core: 2. Of those that a mesh axis runs over, the one named last changes fastest.
Arguments:
- step_queries: bfloat16 [4, 128, 8192], P(None, 'inst', 'tp'), may hold values from -11 to 11
- step_keyvals: bfloat16 [4, 128, 8, 256], P(None, 'inst', 'tp'), may hold values from -9.5 to 9.5
- cache_pages: bfloat16 [2048, 16, 8, 256], P('inst', None, 'tp'), may hold values from -9.5 to 9.5
- block_table: int32 [128, 16], P('inst'), may hold values from 0 to 127, as said below
- context_len: int32 [128], replicated, may hold values from 1 to 256, as said below
- partner: int32 [16], replicated, may hold values from 0 to 15, as said below
- moved_slot: int32 [16], replicated, may hold values from 0 to 7
- prompt_queries: bfloat16 [2048, 8192], P(('inst', 'tp')), may hold values from -11 to 11
- prompt_keyvals: bfloat16 [2048, 8, 256], P(('inst', 'tp')), may hold values from -9.5 to 9.5
- prompt_target: int32 [2048, 1], replicated, may hold values from 0 to 15; in each aligned block of 64 rows (0 to 63, 64 to 127, ...) at most 8 rows name the same one
Outputs:
- decode_output: bfloat16 [4, 128, 8192], P(None, 'inst', 'tp')
- prefill_output: bfloat16 [4096, 8192], P('inst', 'tp')
Inputs may be any that keep to these rules, and one draw needn't show every extreme that they name: partner[partner[i]] = i, and i and partner[i] differ in exactly one bit. `block_table`: the 8 rows of one instance together name each of its 128 pages once. `context_len`: some request holds exactly 256 tokens. `prompt_target`: among the 64 rows of one device no instance is named more than 8 times.
All inputs are finite; a program needn't handle non-finite values.
Results may differ from a plain program's by a relative error of at most 0.0049.
Values may be sent and summed in bfloat16 or wider, within the bound.
A program may use at most 64 MiB of HBM per device.

v0:
```python
import jax
import jax.numpy as jnp
from jax import lax
from jax.sharding import PartitionSpec as P


def swapped(array, axis, bit):
    return lax.ppermute(array, axis, [(i, i ^ 1 << bit) for i in range(lax.axis_size(axis))])


def masked_weights(scores, mask):
    shifted = jnp.where(mask, scores, jnp.float32(-1e30))
    top = jnp.max(shifted, axis=-1, keepdims=True)
    expo = jnp.where(mask, jnp.exp(shifted - top), jnp.float32(0.0))
    total = jnp.sum(expo, axis=-1, keepdims=True)
    total = jnp.where(total > 0, total, jnp.float32(1.0))
    return expo / total


def decode_block(queries, context, lengths, fresh):
    steps, count, width = queries.shape
    kv_heads = context.shape[2]
    head_dim = context.shape[3] // 2
    group = width // (kv_heads * head_dim)
    span = context.shape[1]
    scale = head_dim ** (-0.5)
    query = queries.reshape(steps, count, kv_heads, group, head_dim)
    past = (
        jnp.einsum(
            "trkgd,rckd->trkgc", query, context[..., :head_dim], preferred_element_type=jnp.float32
        )
        * scale
    )
    newer = (
        jnp.einsum(
            "trkgd,urkd->trkgu", query, fresh[..., :head_dim], preferred_element_type=jnp.float32
        )
        * scale
    )
    past_mask = (jnp.arange(span, dtype=jnp.int32)[None, :] < lengths[:, None])[
        None, :, None, None, :
    ]
    step_ids = jnp.arange(steps, dtype=jnp.int32)
    new_mask = (step_ids[None, :] <= step_ids[:, None])[:, None, None, None, :]
    mask = jnp.concatenate(
        [jnp.broadcast_to(past_mask, past.shape), jnp.broadcast_to(new_mask, newer.shape)], axis=-1
    )
    weights = masked_weights(jnp.concatenate([past, newer], axis=-1), mask).astype(jnp.bfloat16)
    out = jnp.einsum(
        "trkgc,rckd->trkgd",
        weights[..., :span],
        context[..., head_dim:],
        preferred_element_type=jnp.float32,
    )
    out = out + jnp.einsum(
        "trkgu,urkd->trkgd",
        weights[..., span:],
        fresh[..., head_dim:],
        preferred_element_type=jnp.float32,
    )
    return out.reshape(steps, count, width).astype(jnp.bfloat16)


def prefill_block(queries, keyvals, valid):
    slots, width = queries.shape
    kv_heads = keyvals.shape[1]
    head_dim = keyvals.shape[2] // 2
    group = width // (kv_heads * head_dim)
    scale = head_dim ** (-0.5)
    query = queries.reshape(slots, kv_heads, group, head_dim)
    block = 512 if slots % 512 == 0 else slots
    pieces = []
    for start in range(0, slots, block):
        finish = start + block
        scores = (
            jnp.einsum(
                "qkgd,ckd->kgqc",
                query[start:finish],
                keyvals[:finish, :, :head_dim],
                preferred_element_type=jnp.float32,
            )
            * scale
        )
        query_pos = jnp.arange(start, finish, dtype=jnp.int32)
        key_pos = jnp.arange(finish, dtype=jnp.int32)
        mask = (valid[None, :finish] & (key_pos[None, :] <= query_pos[:, None]))[None, None]
        weights = masked_weights(scores, jnp.broadcast_to(mask, scores.shape)).astype(jnp.bfloat16)
        out = jnp.einsum(
            "kgqc,ckd->qkgd",
            weights,
            keyvals[:finish, :, head_dim:],
            preferred_element_type=jnp.float32,
        )
        out = jnp.where(valid[start:finish, None, None, None], out, jnp.float32(0.0))
        pieces.append(out.reshape(block, width).astype(jnp.bfloat16))
    return jnp.concatenate(pieces, axis=0)


def local(
    step_queries,
    step_keyvals,
    cache_pages,
    block_table,
    context_len,
    partner,
    moved_slot,
    prompt_queries,
    prompt_keyvals,
    prompt_target,
):
    inst_count = lax.axis_size("inst")
    tp_count = lax.axis_size("tp")
    me_inst = lax.axis_index("inst")
    me_tp = lax.axis_index("tp")
    requests = block_table.shape[0]
    kv_heads = step_keyvals.shape[2]
    head_dim = step_keyvals.shape[3] // 2
    rows_dev = prompt_queries.shape[0]
    capacity = max(2, 2 * rows_dev // inst_count)
    devices = inst_count * tp_count
    targets = prompt_target[:, 0].reshape(devices, rows_dev)
    mine = lax.dynamic_index_in_dim(targets, me_inst * tp_count + me_tp, 0, keepdims=False)
    onehot = (mine[:, None] == jnp.arange(inst_count, dtype=jnp.int32)[None, :]).astype(jnp.int32)
    rank = jnp.sum((jnp.cumsum(onehot, axis=0) - onehot) * onehot, axis=1)
    place = mine * capacity + rank
    dispatch = (
        jnp.arange(inst_count * capacity, dtype=jnp.int32)[:, None] == place[None, :]
    ).astype(jnp.bfloat16)
    send_queries = (
        jnp.dot(dispatch, prompt_queries, preferred_element_type=jnp.float32)
        .astype(jnp.bfloat16)
        .reshape(inst_count, capacity, -1)
    )
    flat_keyvals = prompt_keyvals.reshape(rows_dev, -1)
    send_keyvals = (
        jnp.dot(dispatch, flat_keyvals, preferred_element_type=jnp.float32)
        .astype(jnp.bfloat16)
        .reshape(inst_count, capacity, -1)
    )
    recv_queries, recv_keyvals = (
        lax.all_to_all(
            lax.all_to_all(send_queries, "inst", split_axis=0, concat_axis=0, tiled=True),
            "tp",
            split_axis=2,
            concat_axis=1,
            tiled=True,
        ),
        lax.all_to_all(
            lax.all_to_all(send_keyvals, "inst", split_axis=0, concat_axis=0, tiled=True),
            "tp",
            split_axis=2,
            concat_axis=1,
            tiled=True,
        ),
    )
    gathered = cache_pages[block_table]
    context = gathered.reshape(requests, -1, kv_heads, 2 * head_dim)
    lengths = lax.dynamic_slice_in_dim(context_len, me_inst * requests, requests)
    my_slot = moved_slot[me_inst]
    other = partner[me_inst]
    other_len = context_len[other * requests + moved_slot[other]]
    bit_total = inst_count.bit_length() - 1
    distance = jnp.bitwise_xor(me_inst, other)
    outgoing = lax.dynamic_index_in_dim(context, my_slot, 0, keepdims=False)
    incoming = outgoing
    for bit in range(bit_total):
        arrived = swapped(outgoing, "inst", bit)
        incoming = jnp.where(distance == 1 << bit, arrived, incoming)
    context = lax.dynamic_update_index_in_dim(context, incoming, my_slot, 0)
    lengths = lengths.at[my_slot].set(other_len)
    decode_output = decode_block(step_queries, context, lengths, step_keyvals)
    slots = inst_count * tp_count * capacity
    slot_queries = recv_queries.reshape(slots, -1)
    slot_keyvals = recv_keyvals.reshape(slots, kv_heads, 2 * head_dim)
    counts = jnp.sum((targets == me_inst).astype(jnp.int32), axis=1)
    valid = (jnp.arange(capacity, dtype=jnp.int32)[None, :] < counts[:, None]).reshape(slots)
    prefill_output = prefill_block(slot_queries, slot_keyvals, valid)
    return (decode_output, prefill_output)


def solution(mesh):
    placed = (
        P(None, "inst", "tp"),
        P(None, "inst", "tp", None),
        P("inst", None, "tp", None),
        P("inst", None),
        P(),
        P(),
        P(),
        P(("inst", "tp"), None),
        P(("inst", "tp"), None, None),
        P(),
    )
    return jax.shard_map(
        local,
        mesh=mesh,
        in_specs=placed,
        out_specs=(P(None, "inst", "tp"), P("inst", "tp")),
        check_vma=False,
    )
```

profile of v0, /device:TPU:0, one launch (start us, length us, event | category | flops | bytes accessed | tf_op | source)
XLA Modules:
  0.0 239.2 jit_solution(14162266033931980166)
XLA Ops:
  0.7 0.5 broadcast.97
  1.2 1.4 reduce.5
  2.8 0.2 select_reduce_fusion
  3.0 1.0 copy.115
  4.0 1.1 fusion.8
  5.1 7.5 %all-to-all-start = ((bf16[16,8,2048]{2,1,0:T(8,128)(2,1)}), bf16[16,8,2048]{2,1,0:T(8,128)(2,1)S(1)}, u32[]{:S(2)}, u32[]{:S(2)}) async-start(bf16[16,8,2048]{2,1,0:T(8,128)(2,1)} %fusion.8), calls=%async_computation | async-start | bytes 1048576 | tf_op jit(solution)/shard_map/all_to_all | solution.py:149
  12.6 2.0 fusion.2
  14.6 12.4 %all-to-all-done = bf16[16,8,2048]{2,1,0:T(8,128)(2,1)S(1)} async-done(((bf16[16,8,2048]{2,1,0:T(8,128)(2,1)}), bf16[16,8,2048]{2,1,0:T(8,128)(2,1)S(1)}, u32[]{:S(2)}, u32[]{:S(2)}) %all-to-all-start) | async-done | bytes 524320 | tf_op jit(solution)/shard_map/all_to_all | solution.py:149
  27.0 0.8 copy-done.2
  27.9 4.1 %all-to-all-start.2 = ((bf16[16,8,8192]{2,1,0:T(8,128)(2,1)}), bf16[16,8,8192]{2,1,0:T(8,128)(2,1)S(1)}, u32[]{:S(2)}, u32[]{:S(2)}) async-start(bf16[16,8,8192]{2,1,0:T(8,128)(2,1)} %fusion.2), calls=%async_computation.2 | async-start | bytes 4194304 | tf_op jit(solution)/shard_map/all_to_all | solution.py:142
  32.0 0.6 dynamic_slice.25
  34.0 9.7 %gather_fusion = bf16[128,16,4,256]{3,2,1,0:T(4,128)(2,1)} fusion(bf16[128,16,4,256]{3,2,1,0:T(4,128)(2,1)} %param.14, s32[1024]{0:T(1024)S(1)} %pad_clamp_fusion), kind=kCustom, calls=%fused_computation | custom fusion | bytes 8389120 | tf_op jit(solution)/shard_map/gather | solution.py:156
  43.8 4.7 %copy.84 = bf16[128,16,4,256]{3,1,0,2:T(8,128)(2,1)} copy(bf16[128,16,4,256]{3,2,1,0:T(4,128)(2,1)} %gather_fusion) | data formatting | bytes 8388608 | tf_op jit(solution)/shard_map/gather | solution.py:156
  49.1 0.7 fusion.41
  51.8 1.9 dynamic-slice_bitcast_fusion
  53.7 2.8 %collective-permute-start = (bf16[256,4,256]{2,0,1:T(8,128)(2,1)}, bf16[256,4,256]{2,0,1:T(8,128)(2,1)}, u32[]{:S(2)}, u32[]{:S(2)}) collective-permute-start(bf16[256,4,256]{2,0,1:T(8,128)(2,1)} %dynamic-slice_bitcast_fusion), channel_id=1, source_target_pairs={{0,16},{2,18},{4,20},{6,22},{8,24},{10,26},{12,28},{14,30},{16,0},... | collective-permute-start | bytes 1572872 | tf_op jit(solution)/shard_map/ppermute | solution.py:8
  56.6 1.5 collective-permute-start.1
  58.0 1.5 collective-permute-start.2
  59.5 4.6 %copy.85 = bf16[8,256,4,256]{3,1,2,0:T(8,128)(2,1)} copy(bf16[8,256,4,256]{3,1,0,2:T(8,128)(2,1)} %bitcast.115) | data formatting | bytes 8388608 | tf_op jit(solution)/shard_map/reshape | solution.py:157
  66.1 1.2 fusion.26
  67.3 0.2 fusion.24
  67.5 1.6 copy.90
  69.9 33.8 %collective-permute-done = bf16[256,4,256]{2,0,1:T(8,128)(2,1)} collective-permute-done((bf16[256,4,256]{2,0,1:T(8,128)(2,1)}, bf16[256,4,256]{2,0,1:T(8,128)(2,1)}, u32[]{:S(2)}, u32[]{:S(2)}) %collective-permute-start) | collective-permute-done | bytes 524320 | tf_op jit(solution)/shard_map/ppermute | solution.py:8
  103.7 2.3 bitcast_dynamic-update-slice_fusion
  106.0 3.4 %fusion.15 = f32[4,8,4,8,256]{4,3,0,2,1:T(8,128)} fusion(bf16[8,256,4,256]{3,1,2,0:T(8,128)(2,1)} %bitcast_dynamic-update-slice_fusion, bf16[4,8,4,8,128]{4,1,3,2,0:T(8,128)(2,1)S(1)} %bitcast.126), kind=kOutput, calls=%fused_computation.28 | convolution fusion | flops 67371008 | bytes 3407872 | tf_op jit(solution)/shard_map/trkgd,rckd->trkgc/dot_general | solution.py:29
  109.4 4.2 %copy.94 = bf16[16,8,2048]{0,1,2:T(8,128)(2,1)} copy(bf16[16,8,2048]{2,1,0:T(8,128)(2,1)S(1)} %copy-done.3) | data formatting | bytes 1048576 | tf_op jit(solution)/shard_map/all_to_all | solution.py:149
  113.6 6.7 %reshape.217 = bf16[2,2,65536]{2,1,0:T(2,128)(2,1)} reshape(bf16[2048,8,16]{2,1,0:T(8,128)(2,1)} %bitcast.117) | data formatting | bytes 1048576
  120.3 3.7 %all-to-all-start.1 = ((bf16[2,2,65536]{2,1,0:T(2,128)(2,1)}), bf16[2,2,65536]{2,1,0:T(2,128)(2,1)S(1)}, u32[]{:S(2)}, u32[]{:S(2)}) async-start(bf16[2,2,65536]{2,1,0:T(2,128)(2,1)} %reshape.217), calls=%async_computation.1 | async-start | bytes 1048576 | tf_op jit(solution)/shard_map/all_to_all | solution.py:148
  124.1 4.5 %fusion.42 = (f32[4,8,4,8]{3,0,2,1:T(4,128)S(1)}, f32[4,8,4,8,260]{4,3,0,2,1:T(8,128)}) fusion(f32[4,8,4,8,4]{4,3,0,2,1:T(8,128)S(1)} %copy-done.4, f32[4,8,4,8,256]{4,3,0,2,1:T(8,128)} %fusion.15, pred[4,8,4,8,4]{4,3,0,2,1:T(8,128)(4,1)S(1)} %broadcast_in_dim.79, pred[4,8,4,8,256]{4,3,0,2,1:T(8,128)(4,1)S(1)} %broadcast_in_dim.78), kind=kOutput, calls=%fused_computation.77 | output fusion | flops 1863939 | bytes 2400256 | tf_op jit(solution)/shard_map/sub | solution.py:14
  128.6 13.3 %copy.98 = bf16[16,8,8192]{0,1,2:T(8,128)(2,1)} copy(bf16[16,8,8192]{2,1,0:T(8,128)(2,1)S(1)} %all-to-all-done.2) | data formatting | bytes 4194304 | tf_op jit(solution)/shard_map/all_to_all | solution.py:142
  141.9 26.0 %reshape.215 = bf16[2,2,262144]{2,1,0:T(2,128)(2,1)} reshape(bf16[8192,8,16]{2,1,0:T(8,128)(2,1)} %bitcast.112) | data formatting | bytes 4194304
  167.9 3.8 %all-to-all-start.3 = ((bf16[2,2,262144]{2,1,0:T(2,128)(2,1)}), bf16[2,2,262144]{2,1,0:T(2,128)(2,1)S(1)}, u32[]{:S(2)}, u32[]{:S(2)}) async-start(bf16[2,2,262144]{2,1,0:T(2,128)(2,1)} %reshape.215), calls=%async_computation.3 | async-start | bytes 4194304 | tf_op jit(solution)/shard_map/all_to_all | solution.py:141
  171.6 1.6 divide_convert_fusion.2
  173.3 0.2 convolution_bitcast_fusion
  173.5 2.0 fusion.18
  175.6 0.8 convert_element_type.40
  176.4 4.1 %reshape.218 = bf16[2048,8,16]{2,1,0:T(8,128)(2,1)} reshape(bf16[2,2,65536]{2,1,0:T(2,128)(2,1)S(1)} %all-to-all-done.1) | data formatting | bytes 1048576
  180.5 4.9 %copy.95 = bf16[16,8,2,1024]{3,1,2,0:T(8,128)(2,1)S(1)} copy(bf16[16,8,2,1024]{0,1,3,2:T(8,128)(2,1)} %bitcast.118) | data formatting | bytes 1048576 | tf_op jit(solution)/shard_map/all_to_all | solution.py:148
  185.4 0.4 reshape.187
  185.8 0.2 fusion.39
  186.2 10.4 %all-to-all-done.3 = bf16[2,2,262144]{2,1,0:T(2,128)(2,1)S(1)} async-done(((bf16[2,2,262144]{2,1,0:T(2,128)(2,1)}), bf16[2,2,262144]{2,1,0:T(2,128)(2,1)S(1)}, u32[]{:S(2)}, u32[]{:S(2)}) %all-to-all-start.3) | async-done | bytes 2097184 | tf_op jit(solution)/shard_map/all_to_all | solution.py:141
  196.5 17.7 %reshape.216 = bf16[8192,8,16]{2,1,0:T(8,128)(2,1)} reshape(bf16[2,2,262144]{2,1,0:T(2,128)(2,1)S(1)} %all-to-all-done.3) | data formatting | bytes 4194304
  214.2 16.6 %copy.99 = bf16[16,8,2,4096]{3,1,2,0:T(8,128)(2,1)S(1)} copy(bf16[16,8,2,4096]{0,1,3,2:T(8,128)(2,1)} %bitcast.113) | data formatting | bytes 4194304 | tf_op jit(solution)/shard_map/all_to_all | solution.py:141
  230.8 0.5 copy.116
  231.3 1.4 fusion.11
  232.7 2.7 %fusion.43 = (f32[4,8,256]{2,1,0:T(8,128)S(1)}, f32[4,8,256,256]{2,3,1,0:T(8,128)S(1)}) fusion(f32[4,256,256,8]{2,1,3,0:T(8,128)S(1)} %fusion.11, pred[256,256]{0,1:T(8,128)(4,1)S(1)} %fusion.25), kind=kOutput, calls=%fused_computation.78 | output fusion | flops 14680319 | bytes 16875520 | tf_op jit(solution)/shard_map/sub | solution.py:14
  235.4 1.0 select_convert_fusion
  236.4 2.9 %copy.102 = bf16[256,4096]{1,0:T(8,128)(2,1)} copy(bf16[256,4096]{0,1:T(8,128)(2,1)S(1)} %bitcast.122) | data formatting | bytes 4194304
  (50 shorter events, 1.5 us)
Async XLA Ops:
  0.6 12.0 %copy-start = (bf16[64,8192]{1,0:T(8,128)(2,1)S(1)}, bf16[64,8192]{1,0:T(8,128)(2,1)}, u32[]{:S(2)}) copy-start(bf16[64,8192]{1,0:T(8,128)(2,1)} %param.19) | copy-start | bytes 3145732
  5.1 26.9 %copy-start.10 = (s32[16]{0:T(128)S(1)}, s32[16]{0:T(128)}, u32[]{:S(2)}) copy-start(s32[16]{0:T(128)} %param.17) | copy-start | bytes 196
  5.1 28.8 %copy-start.7 = (s32[8,16]{1,0:T(8,128)S(1)}, s32[8,16]{1,0:T(8,128)}, u32[]{:S(2)}) copy-start(s32[8,16]{1,0:T(8,128)} %param.15) | copy-start | bytes 1540
  5.1 22.0 %all-to-all-start = ((bf16[16,8,2048]{2,1,0:T(8,128)(2,1)}), bf16[16,8,2048]{2,1,0:T(8,128)(2,1)S(1)}, u32[]{:S(2)}, u32[]{:S(2)}) async-start(bf16[16,8,2048]{2,1,0:T(8,128)(2,1)} %fusion.8), calls=%async_computation | async-start | bytes 1048576 | tf_op jit(solution)/shard_map/all_to_all | solution.py:149
  27.0 0.8 copy-start.2
  27.9 92.4 %all-to-all-start.2 = ((bf16[16,8,8192]{2,1,0:T(8,128)(2,1)}), bf16[16,8,8192]{2,1,0:T(8,128)(2,1)S(1)}, u32[]{:S(2)}, u32[]{:S(2)}) async-start(bf16[16,8,8192]{2,1,0:T(8,128)(2,1)} %fusion.2), calls=%async_computation.2 | async-start | bytes 4194304 | tf_op jit(solution)/shard_map/all_to_all | solution.py:142
  43.8 5.4 %copy-start.8 = (s32[16]{0:T(128)S(1)}, s32[16]{0:T(128)}, u32[]{:S(2)}) copy-start(s32[16]{0:T(128)} %param.18) | copy-start | bytes 196
  53.7 12.3 %copy-start.6 = (bf16[4,8,4,256]{3,2,1,0:T(4,128)(2,1)S(1)}, bf16[4,8,4,256]{3,2,1,0:T(4,128)(2,1)}, u32[]{:S(2)}) copy-start(bf16[4,8,4,256]{3,2,1,0:T(4,128)(2,1)} %param.13) | copy-start | bytes 196612
  53.7 12.3 %copy-start.5 = (bf16[4,8,4096]{2,1,0:T(8,128)(2,1)S(1)}, bf16[4,8,4096]{2,1,0:T(8,128)(2,1)}, u32[]{:S(2)}) copy-start(bf16[4,8,4096]{2,1,0:T(8,128)(2,1)} %param.12) | copy-start | bytes 786436
  53.7 15.4 %copy-start.9 = (s32[128]{0:T(128)S(1)}, s32[128]{0:T(128)}, u32[]{:S(2)}) copy-start(s32[128]{0:T(128)} %param.16) | copy-start | bytes 1540
  53.7 50.0 %collective-permute-start = (bf16[256,4,256]{2,0,1:T(8,128)(2,1)}, bf16[256,4,256]{2,0,1:T(8,128)(2,1)}, u32[]{:S(2)}, u32[]{:S(2)}) collective-permute-start(bf16[256,4,256]{2,0,1:T(8,128)(2,1)} %dynamic-slice_bitcast_fusion), channel_id=1, source_target_pairs={{0,16},{2,18},{4,20},{6,22},{8,24},{10,26},{12,28},{14,30},{16,0},... | collective-permute-start | bytes 1572872 | tf_op jit(solution)/shard_map/ppermute | solution.py:8
  56.6 47.1 %collective-permute-start.1 = (bf16[256,4,256]{2,0,1:T(8,128)(2,1)}, bf16[256,4,256]{2,0,1:T(8,128)(2,1)}, u32[]{:S(2)}, u32[]{:S(2)}) collective-permute-start(bf16[256,4,256]{2,0,1:T(8,128)(2,1)} %dynamic-slice_bitcast_fusion), channel_id=1, source_target_pairs={{0,8},{2,10},{4,12},{6,14},{8,0},{10,2},{12,4},{14,6},{16,24},{18,... | collective-permute-start | bytes 1572872 | tf_op jit(solution)/shard_map/ppermute | solution.py:8
  58.0 45.7 %collective-permute-start.2 = (bf16[256,4,256]{2,0,1:T(8,128)(2,1)}, bf16[256,4,256]{2,0,1:T(8,128)(2,1)}, u32[]{:S(2)}, u32[]{:S(2)}) collective-permute-start(bf16[256,4,256]{2,0,1:T(8,128)(2,1)} %dynamic-slice_bitcast_fusion), channel_id=1, source_target_pairs={{0,4},{2,6},{4,0},{6,2},{8,12},{10,14},{12,8},{14,10},{16,20},{18,... | collective-permute-start | bytes 1572872 | tf_op jit(solution)/shard_map/ppermute | solution.py:8
  59.5 44.2 %collective-permute-start.3 = (bf16[256,4,256]{2,0,1:T(8,128)(2,1)}, bf16[256,4,256]{2,0,1:T(8,128)(2,1)}, u32[]{:S(2)}, u32[]{:S(2)}) collective-permute-start(bf16[256,4,256]{2,0,1:T(8,128)(2,1)} %dynamic-slice_bitcast_fusion), channel_id=1, source_target_pairs={{0,2},{2,0},{4,6},{6,4},{8,10},{10,8},{12,14},{14,12},{16,18},{18,... | collective-permute-start | bytes 1572872 | tf_op jit(solution)/shard_map/ppermute | solution.py:8
  66.0 43.4 %copy-start.3 = (bf16[16,8,2048]{2,1,0:T(8,128)(2,1)S(1)}, bf16[16,8,2048]{2,1,0:T(8,128)(2,1)}, u32[]{:S(2)}) copy-start(bf16[16,8,2048]{2,1,0:T(8,128)(2,1)} %copy-done.2) | copy-start | bytes 1572868
  113.6 10.5 %copy-start.4 = (f32[4,8,4,8,4]{4,3,0,2,1:T(8,128)S(1)}, f32[4,8,4,8,4]{4,3,0,2,1:T(8,128)}, u32[]{:S(2)}) copy-start(f32[4,8,4,8,4]{4,3,0,2,1:T(8,128)} %copy.90) | copy-start | bytes 49156
  120.3 47.6 %all-to-all-start.1 = ((bf16[2,2,65536]{2,1,0:T(2,128)(2,1)}), bf16[2,2,65536]{2,1,0:T(2,128)(2,1)S(1)}, u32[]{:S(2)}, u32[]{:S(2)}) async-start(bf16[2,2,65536]{2,1,0:T(2,128)(2,1)} %reshape.217), calls=%async_computation.1 | async-start | bytes 1048576 | tf_op jit(solution)/shard_map/all_to_all | solution.py:148
  167.9 28.7 %all-to-all-start.3 = ((bf16[2,2,262144]{2,1,0:T(2,128)(2,1)}), bf16[2,2,262144]{2,1,0:T(2,128)(2,1)S(1)}, u32[]{:S(2)}, u32[]{:S(2)}) async-start(bf16[2,2,262144]{2,1,0:T(2,128)(2,1)} %reshape.215), calls=%async_computation.3 | async-start | bytes 4194304 | tf_op jit(solution)/shard_map/all_to_all | solution.py:141
  235.4 3.8 %copy-start.1 = (bf16[64,8192]{1,0:T(8,128)(2,1)S(1)}, bf16[64,8192]{1,0:T(8,128)(2,1)}, u32[]{:S(2)}) copy-start(bf16[64,8192]{1,0:T(8,128)(2,1)} %param.19) | copy-start | bytes 3145732
where the time goes:
time: 241 us; the launch traced here: 239 us
  local copies, waits for them, and re-layouts  125 us (52%)
  waiting for transfers between devices  56.6 us (23%)
  starting transfers between devices  24.8 us (10%)
  other arithmetic  13.6 us (6%)
  matrix products  12.3 us (5%)
  between operations  6.88 us (3%)
    unnamed x31, local copies, waits for them, and re-layouts  60.3 us
    ppermute x4, waiting for transfers between devices, swapped(): lax.ppermute(array, axis, [(i, i ^ 1 << bit) for i in range(lax.axis_size...  33.8 us
    all_to_all x1, local copies, waits for them, and re-layouts, local(): lax.all_to_all(lax.all_to_all(send_queries, 'inst', split_axis=0, concat_...  16.6 us
    gather x2, local copies, waits for them, and re-layouts, local(): gathered = cache_pages[block_table]  14.5 us
    all_to_all x1, local copies, waits for them, and re-layouts, local(): lax.all_to_all(send_queries, 'inst', split_axis=0, concat_axis=0, tiled=T...  13.3 us
    all_to_all x1, waiting for transfers between devices, local(): lax.all_to_all(send_keyvals, 'inst', split_axis=0, concat_axis=0, tiled=T...  12.4 us
    all_to_all x1, waiting for transfers between devices, local(): lax.all_to_all(lax.all_to_all(send_queries, 'inst', split_axis=0, concat_...  10.4 us
    all_to_all x1, starting transfers between devices, local(): lax.all_to_all(send_keyvals, 'inst', split_axis=0, concat_axis=0, tiled=T...  7.49 us
  transfers between devices with their start and end apart: 8, of which 3 were waited for; matrix products, arithmetic and copies ran while one was open for 43% of the time, Pallas kernels for 0%

commit v1 on v0

--- a/solution.py
+++ b/solution.py
@@ -1,6 +1,11 @@
+import functools
+import math
+
 import jax
 import jax.numpy as jnp
 from jax import lax
+from jax.experimental import pallas as pl
+from jax.experimental.pallas import tpu as pltpu
 from jax.sharding import PartitionSpec as P
 
 
@@ -96,7 +101,367 @@
     return jnp.concatenate(pieces, axis=0)
 
 
-def local(
+MESH = pl.DeviceIdType.MESH
+NEG = -1e30
+
+
+def fused_kernel(
+    n_inst,
+    n_tp,
+    block_ref,
+    length_ref,
+    partner_ref,
+    moved_ref,
+    step_q_ref,
+    step_kv_ref,
+    cache_hbm,
+    prompt_q_ref,
+    prompt_kv_ref,
+    target_ref,
+    decode_ref,
+    prefill_ref,
+    cache_ref,
+    send_ref,
+    recv_ref,
+    step_ref,
+    context_ref,
+    decoded_ref,
+    move_q_out,
+    move_kv_out,
+    move_q_in,
+    move_kv_in,
+    move_o_out,
+    move_o_in,
+    bias_ref,
+    cache_sem,
+    self_sem,
+    send_sem,
+    recv_sem,
+    move_send_sem,
+    move_recv_sem,
+):
+    f32, bf16 = jnp.float32, jnp.bfloat16
+    me_inst, me_tp = lax.axis_index("inst"), lax.axis_index("tp")
+    me = me_inst * n_tp + me_tp
+    devices = n_inst * n_tp
+    bits = n_inst.bit_length() - 1
+    steps, requests, width = step_q_ref.shape
+    kv_heads, both = step_kv_ref.shape[2:]
+    head = both // 2
+    heads = width // head
+    group = heads // kv_heads
+    rows = prompt_q_ref.shape[0]
+    cap = recv_ref.shape[1]
+    slots = devices * cap
+    pages, page = block_ref.shape[1], cache_ref.shape[1]
+    unit = group * head + both
+    factor = head**-0.5 * math.log2(math.e)
+
+    cache_copy = pltpu.make_async_copy(cache_hbm, cache_ref, cache_sem)
+    cache_copy.start()
+
+    barrier = pltpu.get_barrier_semaphore()
+    for turn in range(1, devices):
+        inst = lax.rem(me_inst + turn // n_tp, n_inst)
+        tp = lax.rem(me_tp + turn % n_tp, n_tp)
+        pl.semaphore_signal(barrier, inc=1, device_id=(inst, tp), device_id_type=MESH)
+
+    for t in range(steps):
+        for h in range(heads):
+            step_ref[t * heads + h] = step_q_ref[t, :, h * head : (h + 1) * head].astype(f32)
+    my_slot = moved_ref[me_inst]
+    distance = partner_ref[me_inst] - me_inst
+    move_q_out[...] = step_ref[:, my_slot, :].astype(bf16)
+    move_kv_out[...] = step_kv_ref[:, my_slot].reshape(steps * kv_heads, both)
+
+    mine = target_ref[pl.ds(pl.multiple_of(me * rows, rows), rows), :].astype(f32)
+    onehot = (
+        mine == lax.broadcasted_iota(jnp.int32, (rows, n_inst), 1).astype(f32)
+    ).astype(f32)
+    earlier = (
+        lax.broadcasted_iota(jnp.int32, (rows, rows), 1)
+        < lax.broadcasted_iota(jnp.int32, (rows, rows), 0)
+    ).astype(bf16)
+    before = jnp.dot(earlier, onehot.astype(bf16), preferred_element_type=f32)
+    rank = jnp.sum(before * onehot, axis=1, keepdims=True)
+    place = mine * cap + rank
+    dispatch = (
+        lax.broadcasted_iota(jnp.int32, (rows, n_inst * cap), 1).astype(f32) == place
+    ).astype(f32)
+    dispatch = jnp.transpose(dispatch).astype(bf16)
+
+    def pack(tp):
+        for h in range(kv_heads):
+            start = (tp * kv_heads + h) * group * head
+            queries = prompt_q_ref[:, start : start + group * head]
+            packed = jnp.dot(dispatch, queries, preferred_element_type=f32)
+            send_ref[tp, :, :, h * unit : h * unit + group * head] = packed.reshape(
+                n_inst, cap, group * head
+            ).astype(bf16)
+            keyvals = prompt_kv_ref[:, tp * kv_heads + h, :]
+            packed = jnp.dot(dispatch, keyvals, preferred_element_type=f32)
+            send_ref[tp, :, :, h * unit + group * head : (h + 1) * unit] = packed.reshape(
+                n_inst, cap, both
+            ).astype(bf16)
+
+    for tp in range(n_tp):
+        pack(tp)
+
+    def neighbour(bit):
+        return me_inst + (1 - 2 * lax.rem(me_inst // (1 << bit), 2)) * (1 << bit)
+
+    def move(bit, source, target, which):
+        return pltpu.make_async_remote_copy(
+            src_ref=source,
+            dst_ref=target.at[bit],
+            send_sem=move_send_sem.at[which, bit],
+            recv_sem=move_recv_sem.at[which, bit],
+            device_id=(neighbour(bit), me_tp),
+            device_id_type=MESH,
+        )
+
+    pl.semaphore_wait(barrier, devices - 1)
+    moves = []
+    for bit in range(bits):
+        moves.append(move(bit, move_q_out, move_q_in, 0))
+        moves.append(move(bit, move_kv_out, move_kv_in, 1))
+    for copy in moves:
+        copy.start()
+
+    own = pltpu.make_async_copy(send_ref.at[me_tp, me_inst], recv_ref.at[me], self_sem)
+    own.start()
+    copies = []
+    order = []
+    half = n_inst // 2
+    for k in range(half):
+        order.extend([half + k, k])
+    for k in order:
+        for t in range(n_tp):
+            if k == 0 and t == 0:
+                continue
+            inst, tp = lax.rem(me_inst + k, n_inst), lax.rem(me_tp + t, n_tp)
+            back_inst = lax.rem(me_inst + n_inst - k, n_inst)
+            back_tp = lax.rem(me_tp + n_tp - t, n_tp)
+            copy = pltpu.make_async_remote_copy(
+                src_ref=send_ref.at[tp, inst],
+                dst_ref=recv_ref.at[me],
+                send_sem=send_sem.at[k * n_tp + t],
+                recv_sem=recv_sem.at[k * n_tp + t],
+                device_id=(inst, tp),
+                device_id_type=MESH,
+            )
+            copy.start()
+            arrival = pltpu.make_async_remote_copy(
+                src_ref=send_ref.at[tp, inst],
+                dst_ref=recv_ref.at[back_inst * n_tp + back_tp],
+                send_sem=send_sem.at[k * n_tp + t],
+                recv_sem=recv_sem.at[k * n_tp + t],
+                device_id=(inst, tp),
+                device_id_type=MESH,
+            )
+            copies.append((copy, arrival))
+
+    here = (target_ref[...] == me_inst).astype(f32).reshape(devices, rows, 1)
+    counts = jnp.sum(here, axis=1, keepdims=True)
+    ranks = lax.broadcasted_iota(jnp.int32, (devices, cap, 1), 1).astype(f32)
+    filled = (ranks < counts).astype(f32).reshape(slots, 1)
+    across = jnp.transpose(jnp.broadcast_to(filled, (slots, 128)))[0:1, :]
+    query_pos = lax.broadcasted_iota(jnp.int32, (slots, slots), 0)
+    key_pos = lax.broadcasted_iota(jnp.int32, (slots, slots), 1)
+    bias_ref[...] = jnp.where((key_pos <= query_pos) & (across > 0), 0.0, NEG)
+
+    cache_copy.wait()
+    for copy in moves:
+        copy.wait()
+    moved_q, moved_kv = move_q_in[0].astype(f32), move_kv_in[0].astype(f32)
+    for bit in range(1, bits):
+        match = (distance == (1 << bit)) | (distance == -(1 << bit))
+        moved_q = jnp.where(match, move_q_in[bit].astype(f32), moved_q)
+        moved_kv = jnp.where(match, move_kv_in[bit].astype(f32), moved_kv)
+    moved_q, moved_kv = moved_q.astype(bf16), moved_kv.astype(bf16)
+
+    queries_all = steps * heads
+    span = pages * page * kv_heads
+    fresh_all = steps * kv_heads
+    query_row = lax.broadcasted_iota(jnp.int32, (queries_all, 1), 0)
+    query_head = lax.rem(query_row, heads) // group
+    query_step = query_row // heads
+    past_col = lax.broadcasted_iota(jnp.int32, (1, span), 1)
+    past_head, past_token = lax.rem(past_col, kv_heads), past_col // kv_heads
+    fresh_col = lax.broadcasted_iota(jnp.int32, (1, fresh_all), 1)
+    fresh_mask = (lax.rem(fresh_col, kv_heads) == query_head) & (
+        fresh_col // kv_heads <= query_step
+    )
+    contract = (((1,), (1,)), ((), ()))
+
+    def decode_slot(slot, carry):
+        for i in range(pages):
+            context_ref[i * page * kv_heads : (i + 1) * page * kv_heads, :] = cache_ref[
+                block_ref[slot, i]
+            ].reshape(page * kv_heads, both)
+        is_moved = slot == my_slot
+        queries = jnp.where(is_moved, moved_q, step_ref[:, slot, :].astype(bf16))
+        fresh = jnp.where(
+            is_moved, moved_kv, step_kv_ref[:, slot].reshape(fresh_all, both)
+        )
+        length = length_ref[me_inst * requests + slot]
+        past = lax.dot_general(
+            queries, context_ref[:, :head], contract, preferred_element_type=f32
+        )
+        newer = lax.dot_general(queries, fresh[:, :head], contract, preferred_element_type=f32)
+        past = jnp.where((past_head == query_head) & (past_token < length), past, NEG)
+        newer = jnp.where(fresh_mask, newer, NEG)
+        top = jnp.maximum(
+            jnp.max(past, axis=1, keepdims=True), jnp.max(newer, axis=1, keepdims=True)
+        )
+        past = jnp.exp2((past - top) * factor)
+        newer = jnp.exp2((newer - top) * factor)
+        total = jnp.sum(past, axis=1, keepdims=True) + jnp.sum(newer, axis=1, keepdims=True)
+        share = 1.0 / total
+        out = jnp.dot(
+            (past * share).astype(bf16), context_ref[:, head:], preferred_element_type=f32
+        )
+        out = out + jnp.dot(
+            (newer * share).astype(bf16), fresh[:, head:], preferred_element_type=f32
+        )
+        decoded_ref[:, slot, :] = out
+        return carry
+
+    lax.fori_loop(0, requests, decode_slot, 0)
+
+    move_o_out[...] = decoded_ref[:, my_slot, :].astype(bf16)
+    returns = [move(bit, move_o_out, move_o_in, 2) for bit in range(bits)]
+    for copy in returns:
+        copy.start()
+    for copy in returns:
+        copy.wait()
+    moved_o = move_o_in[0].astype(f32)
+    for bit in range(1, bits):
+        match = (distance == (1 << bit)) | (distance == -(1 << bit))
+        moved_o = jnp.where(match, move_o_in[bit].astype(f32), moved_o)
+    slot_row = lax.broadcasted_iota(jnp.int32, (requests, 1), 0)
+    for t in range(steps):
+        for h in range(heads):
+            row = t * heads + h
+            decode_ref[t, :, h * head : (h + 1) * head] = jnp.where(
+                slot_row == my_slot, moved_o[row : row + 1, :], decoded_ref[row]
+            ).astype(bf16)
+
+    own.wait()
+    for copy, arrival in copies:
+        copy.wait_send()
+        arrival.wait_recv()
+
+    def prefill_head(h, carry):
+        base = pl.multiple_of(h * unit, 128)
+        keyvals = (
+            recv_ref[:, :, pl.ds(pl.multiple_of(base + group * head, 128), both)]
+            .astype(f32)
+            .reshape(slots, both)
+            .astype(bf16)
+        )
+        keys = keyvals[:, :head]
+        values = jnp.concatenate([keyvals[:, head:], jnp.ones((slots, head), bf16)], axis=1)
+        for g in range(group):
+            queries = (
+                recv_ref[:, :, pl.ds(pl.multiple_of(base + g * head, 128), head)]
+                .astype(f32)
+                .reshape(slots, head)
+                .astype(bf16)
+            )
+            for first in (0, slots // 2):
+                last = first + slots // 2
+                scores = lax.dot_general(
+                    queries[first:last], keys[:last], contract, preferred_element_type=f32
+                )
+                scores = scores + bias_ref[first:last, :last]
+                top = jnp.max(scores, axis=1, keepdims=True)
+                expo = jnp.exp2((scores - top) * factor).astype(bf16)
+                out = jnp.dot(expo, values[:last], preferred_element_type=f32)
+                out = out[:, :head] / out[:, head:]
+                out = jnp.where(filled[first:last] > 0, out, 0.0)
+                prefill_ref[
+                    first:last, pl.ds(pl.multiple_of((h * group + g) * head, 128), head)
+                ] = out.astype(bf16)
+        return carry
+
+    lax.fori_loop(0, kv_heads, prefill_head, 0)
+
+
+def local_fused(
+    step_queries,
+    step_keyvals,
+    cache_pages,
+    block_table,
+    context_len,
+    partner,
+    moved_slot,
+    prompt_queries,
+    prompt_keyvals,
+    prompt_target,
+):
+    n_inst, n_tp = lax.axis_size("inst"), lax.axis_size("tp")
+    devices = n_inst * n_tp
+    bits = n_inst.bit_length() - 1
+    steps, requests, width = step_queries.shape
+    kv_heads, both = step_keyvals.shape[2:]
+    head = both // 2
+    heads = width // head
+    cap = 2 * prompt_queries.shape[0] // n_inst
+    slots = devices * cap
+    columns = width + kv_heads * both
+    span = block_table.shape[1] * cache_pages.shape[1] * kv_heads
+    bf16, f32 = jnp.bfloat16, jnp.float32
+    smem = pl.BlockSpec(memory_space=pltpu.SMEM)
+    vmem = pl.BlockSpec(memory_space=pltpu.VMEM)
+    return pl.pallas_call(
+        functools.partial(fused_kernel, n_inst, n_tp),
+        out_shape=(
+            jax.ShapeDtypeStruct(step_queries.shape, bf16),
+            jax.ShapeDtypeStruct((slots, width), bf16),
+        ),
+        in_specs=[smem] * 4
+        + [vmem, vmem, pl.BlockSpec(memory_space=pl.ANY), vmem, vmem, vmem],
+        out_specs=(vmem, vmem),
+        scratch_shapes=[
+            pltpu.VMEM(cache_pages.shape, bf16),
+            pltpu.VMEM((n_tp, n_inst, cap, columns), bf16),
+            pltpu.VMEM((devices, cap, columns), bf16),
+            pltpu.VMEM((steps * heads, requests, head), f32),
+            pltpu.VMEM((span, both), bf16),
+            pltpu.VMEM((steps * heads, requests, head), f32),
+            pltpu.VMEM((steps * heads, head), bf16),
+            pltpu.VMEM((steps * kv_heads, both), bf16),
+            pltpu.VMEM((bits, steps * heads, head), bf16),
+            pltpu.VMEM((bits, steps * kv_heads, both), bf16),
+            pltpu.VMEM((steps * heads, head), bf16),
+            pltpu.VMEM((bits, steps * heads, head), bf16),
+            pltpu.VMEM((slots, slots), f32),
+            pltpu.SemaphoreType.DMA,
+            pltpu.SemaphoreType.DMA,
+            pltpu.SemaphoreType.DMA((devices,)),
+            pltpu.SemaphoreType.DMA((devices,)),
+            pltpu.SemaphoreType.DMA((3, bits)),
+            pltpu.SemaphoreType.DMA((3, bits)),
+        ],
+        compiler_params=pltpu.CompilerParams(
+            collective_id=0, has_side_effects=True, vmem_limit_bytes=56 << 20
+        ),
+    )(
+        block_table,
+        context_len,
+        partner,
+        moved_slot,
+        step_queries,
+        step_keyvals,
+        cache_pages,
+        prompt_queries,
+        prompt_keyvals,
+        prompt_target,
+    )
+
+
+def local_plain(
     step_queries,
     step_keyvals,
     cache_pages,
@@ -178,6 +543,13 @@
     return (decode_output, prefill_output)
 
 
+def local(*arrays):
+    rows_dev = arrays[7].shape[0]
+    if (2 * rows_dev // lax.axis_size("inst")) % 8:
+        return local_plain(*arrays)
+    return local_fused(*arrays)
+
+
 def solution(mesh):
     placed = (
         P(None, "inst", "tp"),

time: 241 us -> 85.6 us (0.36)
  local copies, waits for them, and re-layouts: 125 us -> 6.83 us
  Pallas kernels: 0 us -> 77.9 us
  waiting for transfers between devices: 56.6 us -> 0 us
  starting transfers between devices: 24.8 us -> 0 us
  other arithmetic: 13.6 us -> 0 us
  matrix products: 12.3 us -> 0 us
  between operations: 6.88 us -> 0.64 us
    pallas_call x0 -> x1, Pallas kernels: none -> 77.9 us  [local_fused(): pl.pallas_call(functools.partial(fused_kernel, n_inst, n_tp), out_shape=(...]
    unnamed x31 -> x3, local copies, waits for them, and re-layouts: 60.3 us -> 6.83 us
    all_to_all x4 -> x0, local copies, waits for them, and re-layouts: 39.1 us -> none  [the longest x1 16.6 us: local(): lax.all_to_all(lax.all_to_all(send_queries, 'inst', split_axis=0, concat_...]
    ppermute x4 -> x0, waiting for transfers between devices: 33.8 us -> none  [swapped(): lax.ppermute(array, axis, [(i, i ^ 1 << bit) for i in range(lax.axis_size...]
    all_to_all x4 -> x0, waiting for transfers between devices: 22.8 us -> none  [the longest x1 12.4 us: local(): lax.all_to_all(send_keyvals, 'inst', split_axis=0, concat_axis=0, tiled=T...]
    all_to_all x4 -> x0, starting transfers between devices: 19 us -> none  [the longest x1 7.49 us: local(): lax.all_to_all(send_keyvals, 'inst', split_axis=0, concat_axis=0, tiled=T...]
    gather x2 -> x0, local copies, waits for them, and re-layouts: 14.5 us -> none  [local(): gathered = cache_pages[block_table]]
    dot_general x8 -> x0, matrix products: 12.3 us -> none  [the longest x1 3.37 us: decode_block(): jnp.einsum('trkgd,rckd->trkgc', query, context[..., :head_dim], preferred...]
  transfers between devices with their start and end apart: 8 -> 0, of which waited for: 3 -> 0; matrix products, arithmetic and copies ran while one was open for 43% -> 0% of each run, Pallas kernels for 0% -> 0%
where the time goes in v1:
time: 85.6 us; the launch traced here: 85.3 us
  Pallas kernels  77.9 us (91%)
  local copies, waits for them, and re-layouts  6.83 us (8%)
    pallas_call x1, Pallas kernels, local_fused(): pl.pallas_call(functools.partial(fused_kernel, n_inst, n_tp), out_shape=(...  77.9 us
    unnamed x3, local copies, waits for them, and re-layouts  6.83 us

profile of v1, /device:TPU:0, one launch (start us, length us, event | category | flops | bytes accessed | tf_op | source)
XLA Modules:
  0.0 85.3 jit_solution(1944810309413041904)
XLA Ops:
  0.6 2.0 %copy.12.target_ref = s32[2048,1]{1,0:T(8,128)} copy(s32[2048,1]{0,1:T(1,128)} %param.19) | data formatting | bytes 16384 | tf_op args[9]
  2.7 77.9 %shard_map.113 = (bf16[4,8,4096]{2,1,0:T(8,128)(2,1)}, bf16[256,4096]{1,0:T(8,128)(2,1)}) custom-call(s32[8,16]{1,0:T(8,128)} %block_ref.1, s32[128]{0:T(128)} %length_ref.1, s32[16]{0:T(128)} %partner_ref.1, s32[16]{0:T(128)} %moved_ref.1, bf16[4,8,4096]{2,1,0:T(8,128)(2,1)} %step_q_ref.1, bf16[4,8,4,256]{3,2,1,0:T(4,128)(2,1)} %step_kv_ref.1, ...), custom_call_target="tpu_custom_call" | custom-call | tf_op jit(solution)/shard_map/pallas_call | solution.py:417
  80.5 1.7 %copy.15 = bf16[4,8,4096]{2,1,0:T(8,128)(2,1)} copy(bf16[4,8,4096]{2,1,0:T(8,128)(2,1)} %get-tuple-element.4) | data formatting | bytes 524288
  82.2 3.1 %copy.16 = bf16[256,4096]{1,0:T(8,128)(2,1)} copy(bf16[256,4096]{1,0:T(8,128)(2,1)} %get-tuple-element.5) | data formatting | bytes 4194304

commit v2 on v1

--- a/solution.py
+++ b/solution.py
@@ -115,12 +115,13 @@
     step_q_ref,
     step_kv_ref,
     cache_hbm,
-    prompt_q_ref,
+    prompt_q_hbm,
     prompt_kv_ref,
     target_ref,
     decode_ref,
     prefill_ref,
     cache_ref,
+    prompt_q_ref,
     send_ref,
     recv_ref,
     step_ref,
@@ -133,7 +134,11 @@
     move_o_out,
     move_o_in,
     bias_ref,
+    filled_ref,
+    part_ref,
+    part_top_ref,
     cache_sem,
+    prompt_sem,
     self_sem,
     send_sem,
     recv_sem,
@@ -150,13 +155,23 @@
     head = both // 2
     heads = width // head
     group = heads // kv_heads
-    rows = prompt_q_ref.shape[0]
+    rows = prompt_q_ref.shape[1]
     cap = recv_ref.shape[1]
     slots = devices * cap
     pages, page = block_ref.shape[1], cache_ref.shape[1]
     unit = group * head + both
     factor = head**-0.5 * math.log2(math.e)
 
+    prompt_copies = [
+        pltpu.make_async_copy(
+            prompt_q_hbm.at[:, tp * width : (tp + 1) * width],
+            prompt_q_ref.at[tp],
+            prompt_sem.at[tp],
+        )
+        for tp in range(n_tp)
+    ]
+    for copy in prompt_copies:
+        copy.start()
     cache_copy = pltpu.make_async_copy(cache_hbm, cache_ref, cache_sem)
     cache_copy.start()
 
@@ -174,26 +189,27 @@
     move_q_out[...] = step_ref[:, my_slot, :].astype(bf16)
     move_kv_out[...] = step_kv_ref[:, my_slot].reshape(steps * kv_heads, both)
 
-    mine = target_ref[pl.ds(pl.multiple_of(me * rows, rows), rows), :].astype(f32)
-    onehot = (
-        mine == lax.broadcasted_iota(jnp.int32, (rows, n_inst), 1).astype(f32)
+    lanes = n_tp * rows
+    mine = target_ref[pl.ds(me_inst, 1), :]
+    onehot = (lax.broadcasted_iota(jnp.int32, (n_inst, lanes), 0) == mine).astype(f32)
+    row_from = lax.broadcasted_iota(jnp.int32, (lanes, lanes), 0)
+    row_to = lax.broadcasted_iota(jnp.int32, (lanes, lanes), 1)
+    earlier = ((row_from < row_to) & (row_from // rows == row_to // rows)).astype(bf16)
+    before = jnp.dot(onehot.astype(bf16), earlier, preferred_element_type=f32)
+    rank = jnp.sum(before * onehot, axis=0, keepdims=True)
+    place = mine.astype(f32) * cap + rank
+    both_rows = (
+        lax.broadcasted_iota(jnp.int32, (n_inst * cap, lanes), 0).astype(f32) == place
     ).astype(f32)
-    earlier = (
-        lax.broadcasted_iota(jnp.int32, (rows, rows), 1)
-        < lax.broadcasted_iota(jnp.int32, (rows, rows), 0)
-    ).astype(bf16)
-    before = jnp.dot(earlier, onehot.astype(bf16), preferred_element_type=f32)
-    rank = jnp.sum(before * onehot, axis=1, keepdims=True)
-    place = mine * cap + rank
-    dispatch = (
-        lax.broadcasted_iota(jnp.int32, (rows, n_inst * cap), 1).astype(f32) == place
-    ).astype(f32)
-    dispatch = jnp.transpose(dispatch).astype(bf16)
+    dispatch = both_rows[:, :rows]
+    for tp in range(1, n_tp):
+        dispatch = jnp.where(me_tp == tp, both_rows[:, tp * rows : (tp + 1) * rows], dispatch)
+    dispatch = dispatch.astype(bf16)
 
     def pack(tp):
         for h in range(kv_heads):
-            start = (tp * kv_heads + h) * group * head
-            queries = prompt_q_ref[:, start : start + group * head]
+            start = h * group * head
+            queries = prompt_q_ref[tp, :, start : start + group * head]
             packed = jnp.dot(dispatch, queries, preferred_element_type=f32)
             send_ref[tp, :, :, h * unit : h * unit + group * head] = packed.reshape(
                 n_inst, cap, group * head
@@ -204,9 +220,6 @@
                 n_inst, cap, both
             ).astype(bf16)
 
-    for tp in range(n_tp):
-        pack(tp)
-
     def neighbour(bit):
         return me_inst + (1 - 2 * lax.rem(me_inst // (1 << bit), 2)) * (1 << bit)
 
@@ -220,52 +233,54 @@
             device_id_type=MESH,
         )
 
-    pl.semaphore_wait(barrier, devices - 1)
     moves = []
     for bit in range(bits):
         moves.append(move(bit, move_q_out, move_q_in, 0))
         moves.append(move(bit, move_kv_out, move_kv_in, 1))
-    for copy in moves:
-        copy.start()
-
+
+    def shipment(inst, tp, source):
+        return pltpu.make_async_remote_copy(
+            src_ref=send_ref.at[tp, inst],
+            dst_ref=recv_ref.at[source],
+            send_sem=send_sem.at[inst * n_tp + tp],
+            recv_sem=recv_sem.at[source],
+            device_id=(inst, tp),
+            device_id_type=MESH,
+        )
+
+    half = n_inst // 2
+    order = []
+    for j in range(half):
+        order.extend([half + j, j])
+    for tp in range(n_tp):
+        prompt_copies[tp].wait()
+        pack(tp)
+        if tp == 0:
+            pl.semaphore_wait(barrier, devices - 1)
+            for copy in moves:
+                copy.start()
+        for j in order:
+            inst = lax.rem(me_inst + j, n_inst)
+            if j:
+                shipment(inst, tp, me).start()
+            else:
+                pl.when(me_tp != tp)(lambda: shipment(me_inst, tp, me).start())
     own = pltpu.make_async_copy(send_ref.at[me_tp, me_inst], recv_ref.at[me], self_sem)
     own.start()
-    copies = []
-    order = []
-    half = n_inst // 2
-    for k in range(half):
-        order.extend([half + k, k])
-    for k in order:
-        for t in range(n_tp):
-            if k == 0 and t == 0:
-                continue
-            inst, tp = lax.rem(me_inst + k, n_inst), lax.rem(me_tp + t, n_tp)
-            back_inst = lax.rem(me_inst + n_inst - k, n_inst)
-            back_tp = lax.rem(me_tp + n_tp - t, n_tp)
-            copy = pltpu.make_async_remote_copy(
-                src_ref=send_ref.at[tp, inst],
-                dst_ref=recv_ref.at[me],
-                send_sem=send_sem.at[k * n_tp + t],
-                recv_sem=recv_sem.at[k * n_tp + t],
-                device_id=(inst, tp),
-                device_id_type=MESH,
-            )
-            copy.start()
-            arrival = pltpu.make_async_remote_copy(
-                src_ref=send_ref.at[tp, inst],
-                dst_ref=recv_ref.at[back_inst * n_tp + back_tp],
-                send_sem=send_sem.at[k * n_tp + t],
-                recv_sem=recv_sem.at[k * n_tp + t],
-                device_id=(inst, tp),
-                device_id_type=MESH,
-            )
-            copies.append((copy, arrival))
-
-    here = (target_ref[...] == me_inst).astype(f32).reshape(devices, rows, 1)
-    counts = jnp.sum(here, axis=1, keepdims=True)
-    ranks = lax.broadcasted_iota(jnp.int32, (devices, cap, 1), 1).astype(f32)
-    filled = (ranks < counts).astype(f32).reshape(slots, 1)
-    across = jnp.transpose(jnp.broadcast_to(filled, (slots, 128)))[0:1, :]
+
+    here = (target_ref[...] == me_inst).astype(bf16)
+    slot = lax.broadcasted_iota(jnp.int32, (slots, 1), 0)
+    spread = (
+        slot // (n_tp * cap) == lax.broadcasted_iota(jnp.int32, (slots, n_inst), 1)
+    ).astype(bf16)
+    named = jnp.dot(spread, here, preferred_element_type=f32)
+    lane = lax.broadcasted_iota(jnp.int32, (slots, lanes), 1)
+    named = jnp.where(lane // rows == lax.rem(slot // cap, n_tp), named, 0.0)
+    counts = jnp.sum(named, axis=1, keepdims=True)
+    filled = (lax.rem(slot, cap).astype(f32) < counts).astype(f32)
+    filled = jnp.broadcast_to(filled, (slots, head))
+    filled_ref[...] = filled
+    across = jnp.transpose(filled)[0:1, :]
     query_pos = lax.broadcasted_iota(jnp.int32, (slots, slots), 0)
     key_pos = lax.broadcasted_iota(jnp.int32, (slots, slots), 1)
     bias_ref[...] = jnp.where((key_pos <= query_pos) & (across > 0), 0.0, NEG)
@@ -347,45 +362,107 @@
                 slot_row == my_slot, moved_o[row : row + 1, :], decoded_ref[row]
             ).astype(bf16)
 
+    size = slots // 2
+    local_inst = lax.rem(me_inst, half)
+    near_base = me_inst - local_inst
+    far_base = half - near_base
+    is_low = me_inst < half
+
+    def take(part, column, count):
+        first = part * (devices // 2)
+        rows_in = recv_ref[
+            first : first + devices // 2, :, pl.ds(pl.multiple_of(column, 128), count)
+        ]
+        return rows_in.astype(f32).reshape(size, count).astype(bf16)
+
+    def keys_of(part, h):
+        keyvals = take(part, h * unit + group * head, both)
+        ones = jnp.ones((size, head), bf16)
+        return keyvals[:, :head], jnp.concatenate([keyvals[:, head:], ones], axis=1)
+
+    def attend(part, h, g, keys, values, first):
+        queries = take(part, h * unit + g * head, head)
+        scores = lax.dot_general(queries, keys, contract, preferred_element_type=f32)
+        scores = scores + bias_ref[part * size : (part + 1) * size, pl.ds(first, keys.shape[0])]
+        top = jnp.max(scores, axis=1, keepdims=True)
+        return scores, top
+
+    def finish(part, h, g, out):
+        out = out[:, :head] / out[:, head:]
+        out = jnp.where(filled_ref[part * size : (part + 1) * size, :] > 0, out, 0.0)
+        column = pl.multiple_of((h * group + g) * head, 128)
+        prefill_ref[part * size : (part + 1) * size, pl.ds(column, head)] = out.astype(bf16)
+
+    def whole(part, h, g, keys, values):
+        scores, top = attend(part, h, g, keys, values, 0)
+        expo = jnp.exp2((scores - top) * factor).astype(bf16)
+        finish(part, h, g, jnp.dot(expo, values, preferred_element_type=f32))
+
+    def lower(h, carry):
+        keys, values = keys_of(0, h)
+        for g in range(group):
+            whole(0, h, g, keys, values)
+        return carry
+
+    def upper_alone(h, carry):
+        keys, values = keys_of(1, h)
+        for g in range(group):
+            scores, top = attend(1, h, g, keys, values, size)
+            expo = jnp.exp2((scores - top) * factor).astype(bf16)
+            part_ref[h * group + g] = jnp.dot(expo, values, preferred_element_type=f32)
+            part_top_ref[h * group + g] = jnp.broadcast_to(top, (size, head))
+        return carry
+
+    def upper_all(h, carry):
+        keys_0, values_0 = keys_of(0, h)
+        keys_1, values_1 = keys_of(1, h)
+        keys = jnp.concatenate([keys_0, keys_1], axis=0)
+        values = jnp.concatenate([values_0, values_1], axis=0)
+        for g in range(group):
+            whole(1, h, g, keys, values)
+        return carry
+
+    def lower_then_upper(h, carry):
+        keys, values = keys_of(0, h)
+        for g in range(group):
+            whole(0, h, g, keys, values)
+            scores, top = attend(1, h, g, keys, values, 0)
+            before_top = part_top_ref[h * group + g][:, :1]
+            new_top = jnp.maximum(top, before_top)
+            expo = jnp.exp2((scores - new_top) * factor).astype(bf16)
+            out = jnp.dot(expo, values, preferred_element_type=f32)
+            out = out + part_ref[h * group + g] * jnp.exp2((before_top - new_top) * factor)
+            finish(1, h, g, out)
+        return carry
+
+    def loop(body):
+        def run():
+            lax.fori_loop(0, kv_heads, body, 0)
+
+        return run
+
     own.wait()
-    for copy, arrival in copies:
-        copy.wait_send()
-        arrival.wait_recv()
-
-    def prefill_head(h, carry):
-        base = pl.multiple_of(h * unit, 128)
-        keyvals = (
-            recv_ref[:, :, pl.ds(pl.multiple_of(base + group * head, 128), both)]
-            .astype(f32)
-            .reshape(slots, both)
-            .astype(bf16)
-        )
-        keys = keyvals[:, :head]
-        values = jnp.concatenate([keyvals[:, head:], jnp.ones((slots, head), bf16)], axis=1)
-        for g in range(group):
-            queries = (
-                recv_ref[:, :, pl.ds(pl.multiple_of(base + g * head, 128), head)]
-                .astype(f32)
-                .reshape(slots, head)
-                .astype(bf16)
-            )
-            for first in (0, slots // 2):
-                last = first + slots // 2
-                scores = lax.dot_general(
-                    queries[first:last], keys[:last], contract, preferred_element_type=f32
-                )
-                scores = scores + bias_ref[first:last, :last]
-                top = jnp.max(scores, axis=1, keepdims=True)
-                expo = jnp.exp2((scores - top) * factor).astype(bf16)
-                out = jnp.dot(expo, values[:last], preferred_element_type=f32)
-                out = out[:, :head] / out[:, head:]
-                out = jnp.where(filled[first:last] > 0, out, 0.0)
-                prefill_ref[
-                    first:last, pl.ds(pl.multiple_of((h * group + g) * head, 128), head)
-                ] = out.astype(bf16)
-        return carry
-
-    lax.fori_loop(0, kv_heads, prefill_head, 0)
+    for j in range(half):
+        for t in range(n_tp):
+            if j or t:
+                inst = near_base + lax.rem(local_inst + j, half)
+                source = inst * n_tp + lax.rem(me_tp + t, n_tp)
+                shipment(me_inst, me_tp, source).wait_recv()
+    pl.when(is_low)(loop(lower))
+    pl.when(jnp.logical_not(is_low))(loop(upper_alone))
+    for j in range(half):
+        for t in range(n_tp):
+            inst = far_base + lax.rem(local_inst + j, half)
+            source = inst * n_tp + lax.rem(me_tp + t, n_tp)
+            shipment(me_inst, me_tp, source).wait_recv()
+    pl.when(is_low)(loop(upper_all))
+    pl.when(jnp.logical_not(is_low))(loop(lower_then_upper))
+
+    for j in range(n_inst):
+        for t in range(n_tp):
+            if j or t:
+                inst, tp = lax.rem(me_inst + j, n_inst), lax.rem(me_tp + t, n_tp)
+                shipment(inst, tp, me).wait_send()
 
 
 def local_fused(
@@ -414,17 +491,19 @@
     bf16, f32 = jnp.bfloat16, jnp.float32
     smem = pl.BlockSpec(memory_space=pltpu.SMEM)
     vmem = pl.BlockSpec(memory_space=pltpu.VMEM)
+    hbm = pl.BlockSpec(memory_space=pltpu.HBM)
     return pl.pallas_call(
         functools.partial(fused_kernel, n_inst, n_tp),
         out_shape=(
-            jax.ShapeDtypeStruct(step_queries.shape, bf16),
-            jax.ShapeDtypeStruct((slots, width), bf16),
+            pltpu.VMEM(step_queries.shape, bf16),
+            pltpu.VMEM((slots, width), bf16),
         ),
         in_specs=[smem] * 4
-        + [vmem, vmem, pl.BlockSpec(memory_space=pl.ANY), vmem, vmem, vmem],
+        + [vmem, vmem, hbm, hbm, vmem, vmem],
         out_specs=(vmem, vmem),
         scratch_shapes=[
             pltpu.VMEM(cache_pages.shape, bf16),
+            pltpu.VMEM((n_tp, prompt_queries.shape[0], width), bf16),
             pltpu.VMEM((n_tp, n_inst, cap, columns), bf16),
             pltpu.VMEM((devices, cap, columns), bf16),
             pltpu.VMEM((steps * heads, requests, head), f32),
@@ -437,7 +516,11 @@
             pltpu.VMEM((steps * heads, head), bf16),
             pltpu.VMEM((bits, steps * heads, head), bf16),
             pltpu.VMEM((slots, slots), f32),
+            pltpu.VMEM((slots, head), f32),
+            pltpu.VMEM((heads, slots // 2, both), f32),
+            pltpu.VMEM((heads, slots // 2, head), f32),
             pltpu.SemaphoreType.DMA,
+            pltpu.SemaphoreType.DMA((n_tp,)),
             pltpu.SemaphoreType.DMA,
             pltpu.SemaphoreType.DMA((devices,)),
             pltpu.SemaphoreType.DMA((devices,)),
@@ -445,7 +528,7 @@
             pltpu.SemaphoreType.DMA((3, bits)),
         ],
         compiler_params=pltpu.CompilerParams(
-            collective_id=0, has_side_effects=True, vmem_limit_bytes=56 << 20
+            collective_id=0, has_side_effects=True, vmem_limit_bytes=58 << 20
         ),
     )(
         block_table,
@@ -457,7 +540,7 @@
         cache_pages,
         prompt_queries,
         prompt_keyvals,
-        prompt_target,
+        prompt_target.reshape(n_inst, -1),
     )
 
 

time: 85.6 us -> 98.5 us (1.15)
  the two profiles are of different devices: /device:TPU:0 before, /device:TPU:28 now
where the time goes in v2:
time: 98.5 us; the launch traced here: 98.4 us
  Pallas kernels  95.7 us (97%)
  local copies, waits for them, and re-layouts  2.02 us (2%)
    pallas_call x1, Pallas kernels, local_fused(): pl.pallas_call(functools.partial(fused_kernel, n_inst, n_tp), out_shape=(...  95.7 us
    unnamed x2, local copies, waits for them, and re-layouts  2.02 us

profile of v2, /device:TPU:28, one launch (start us, length us, event | category | flops | bytes accessed | tf_op | source)
XLA Modules:
  0.0 98.4 jit_solution(297857761753310556)
XLA Ops:
  0.6 95.7 %shard_map.113 = (bf16[4,8,4096]{2,1,0:T(8,128)(2,1)S(1)}, bf16[256,4096]{1,0:T(8,128)(2,1)S(1)}) custom-call(s32[8,16]{1,0:T(8,128)} %block_ref.1, s32[128]{0:T(128)} %length_ref.1, s32[16]{0:T(128)} %partner_ref.1, s32[16]{0:T(128)} %moved_ref.1, bf16[4,8,4096]{2,1,0:T(8,128)(2,1)} %step_q_ref.1, bf16[4,8,4,256]{3,2,1,0:T(4,128)(2,1)} %step_kv_ref.1, ...), custom_call_target="tpu_custom_call" | custom-call | tf_op jit(solution)/shard_map/pallas_call | solution.py:495
  96.3 0.7 copy.14
  97.0 1.3 %copy.15 = bf16[256,4096]{1,0:T(8,128)(2,1)} copy(bf16[256,4096]{1,0:T(8,128)(2,1)S(1)} %get-tuple-element.3) | data formatting | bytes 4194304

commit v3 on v2

--- a/solution.py
+++ b/solution.py
@@ -302,7 +302,13 @@
     query_head = lax.rem(query_row, heads) // group
     query_step = query_row // heads
     past_col = lax.broadcasted_iota(jnp.int32, (1, span), 1)
-    past_head, past_token = lax.rem(past_col, kv_heads), past_col // kv_heads
+    past_head = lax.rem(past_col, kv_heads)
+    page_row = lax.rem(past_col, page * kv_heads)
+    past_token = (
+        past_col // (page * kv_heads) * page
+        + page_row // (2 * kv_heads)
+        + lax.rem(page_row // kv_heads, 2) * (page // 2)
+    )
     fresh_col = lax.broadcasted_iota(jnp.int32, (1, fresh_all), 1)
     fresh_mask = (lax.rem(fresh_col, kv_heads) == query_head) & (
         fresh_col // kv_heads <= query_step
@@ -311,9 +317,11 @@
 
     def decode_slot(slot, carry):
         for i in range(pages):
-            context_ref[i * page * kv_heads : (i + 1) * page * kv_heads, :] = cache_ref[
-                block_ref[slot, i]
-            ].reshape(page * kv_heads, both)
+            tokens = cache_ref[block_ref[slot, i]].astype(f32)
+            paired = jnp.concatenate([tokens[: page // 2], tokens[page // 2 :]], axis=1)
+            context_ref[i * page * kv_heads : (i + 1) * page * kv_heads, :] = paired.reshape(
+                page * kv_heads, both
+            ).astype(bf16)
         is_moved = slot == my_slot
         queries = jnp.where(is_moved, moved_q, step_ref[:, slot, :].astype(bf16))
         fresh = jnp.where(
@@ -380,37 +388,41 @@
         ones = jnp.ones((size, head), bf16)
         return keyvals[:, :head], jnp.concatenate([keyvals[:, head:], ones], axis=1)
 
-    def attend(part, h, g, keys, values, first):
-        queries = take(part, h * unit + g * head, head)
+    def attend(part, h, keys, first):
+        queries = take(part, h * unit, group * head)
+        queries = jnp.concatenate(
+            [queries[:, g * head : (g + 1) * head] for g in range(group)], axis=0
+        )
         scores = lax.dot_general(queries, keys, contract, preferred_element_type=f32)
-        scores = scores + bias_ref[part * size : (part + 1) * size, pl.ds(first, keys.shape[0])]
-        top = jnp.max(scores, axis=1, keepdims=True)
-        return scores, top
-
-    def finish(part, h, g, out):
+        count = keys.shape[0]
+        bias = bias_ref[part * size : (part + 1) * size, first : first + count]
+        scores = (scores.reshape(group, size, count) + bias[None]).reshape(group * size, count)
+        return scores, jnp.max(scores, axis=1, keepdims=True)
+
+    def weigh(scores, top, values):
+        expo = jnp.exp2((scores - top) * factor).astype(bf16)
+        return jnp.dot(expo, values, preferred_element_type=f32)
+
+    def finish(part, h, out):
         out = out[:, :head] / out[:, head:]
-        out = jnp.where(filled_ref[part * size : (part + 1) * size, :] > 0, out, 0.0)
-        column = pl.multiple_of((h * group + g) * head, 128)
-        prefill_ref[part * size : (part + 1) * size, pl.ds(column, head)] = out.astype(bf16)
-
-    def whole(part, h, g, keys, values):
-        scores, top = attend(part, h, g, keys, values, 0)
-        expo = jnp.exp2((scores - top) * factor).astype(bf16)
-        finish(part, h, g, jnp.dot(expo, values, preferred_element_type=f32))
+        keep = filled_ref[part * size : (part + 1) * size, :] > 0
+        for g in range(group):
+            column = pl.multiple_of((h * group + g) * head, 128)
+            prefill_ref[part * size : (part + 1) * size, pl.ds(column, head)] = jnp.where(
+                keep, out[g * size : (g + 1) * size], 0.0
+            ).astype(bf16)
 
     def lower(h, carry):
         keys, values = keys_of(0, h)
-        for g in range(group):
-            whole(0, h, g, keys, values)
+        scores, top = attend(0, h, keys, 0)
+        finish(0, h, weigh(scores, top, values))
         return carry
 
     def upper_alone(h, carry):
         keys, values = keys_of(1, h)
-        for g in range(group):
-            scores, top = attend(1, h, g, keys, values, size)
-            expo = jnp.exp2((scores - top) * factor).astype(bf16)
-            part_ref[h * group + g] = jnp.dot(expo, values, preferred_element_type=f32)
-            part_top_ref[h * group + g] = jnp.broadcast_to(top, (size, head))
+        scores, top = attend(1, h, keys, size)
+        part_ref[h] = weigh(scores, top, values)
+        part_top_ref[h] = jnp.broadcast_to(top, (group * size, head))
         return carry
 
     def upper_all(h, carry):
@@ -418,21 +430,21 @@
         keys_1, values_1 = keys_of(1, h)
         keys = jnp.concatenate([keys_0, keys_1], axis=0)
         values = jnp.concatenate([values_0, values_1], axis=0)
-        for g in range(group):
-            whole(1, h, g, keys, values)
+        scores, top = attend(1, h, keys, 0)
+        finish(1, h, weigh(scores, top, values))
         return carry
 
     def lower_then_upper(h, carry):
         keys, values = keys_of(0, h)
-        for g in range(group):
-            whole(0, h, g, keys, values)
-            scores, top = attend(1, h, g, keys, values, 0)
-            before_top = part_top_ref[h * group + g][:, :1]
-            new_top = jnp.maximum(top, before_top)
-            expo = jnp.exp2((scores - new_top) * factor).astype(bf16)
-            out = jnp.dot(expo, values, preferred_element_type=f32)
-            out = out + part_ref[h * group + g] * jnp.exp2((before_top - new_top) * factor)
-            finish(1, h, g, out)
+        scores, top = attend(0, h, keys, 0)
+        finish(0, h, weigh(scores, top, values))
+        scores, top = attend(1, h, keys, 0)
+        old_top = part_top_ref[h]
+        new_top = jnp.maximum(old_top, top)
+        out = weigh(scores, new_top[:, :1], values)
+        decay = jnp.exp2((old_top - new_top) * factor)
+        out = out + part_ref[h] * jnp.concatenate([decay, decay], axis=1)
+        finish(1, h, out)
         return carry
 
     def loop(body):
@@ -517,8 +529,8 @@
             pltpu.VMEM((bits, steps * heads, head), bf16),
             pltpu.VMEM((slots, slots), f32),
             pltpu.VMEM((slots, head), f32),
-            pltpu.VMEM((heads, slots // 2, both), f32),
-            pltpu.VMEM((heads, slots // 2, head), f32),
+            pltpu.VMEM((kv_heads, heads // kv_heads * slots // 2, both), f32),
+            pltpu.VMEM((kv_heads, heads // kv_heads * slots // 2, head), f32),
             pltpu.SemaphoreType.DMA,
             pltpu.SemaphoreType.DMA((n_tp,)),
             pltpu.SemaphoreType.DMA,

time: 98.5 us -> 79.6 us (0.81)
  Pallas kernels: 95.7 us -> 76.8 us
    pallas_call x1, Pallas kernels: 95.7 us -> 76.8 us  [local_fused(): pl.pallas_call(functools.partial(fused_kernel, n_inst, n_tp), out_shape=(...]
where the time goes in v3:
time: 79.6 us; the launch traced here: 79.4 us
  Pallas kernels  76.8 us (96%)
  local copies, waits for them, and re-layouts  2.02 us (3%)
    pallas_call x1, Pallas kernels, local_fused(): pl.pallas_call(functools.partial(fused_kernel, n_inst, n_tp), out_shape=(...  76.8 us
    unnamed x2, local copies, waits for them, and re-layouts  2.02 us

profile of v3, /device:TPU:28, one launch (start us, length us, event | category | flops | bytes accessed | tf_op | source)
XLA Modules:
  0.0 79.4 jit_solution(17876276476066429919)
XLA Ops:
  0.6 76.8 %shard_map.113 = (bf16[4,8,4096]{2,1,0:T(8,128)(2,1)S(1)}, bf16[256,4096]{1,0:T(8,128)(2,1)S(1)}) custom-call(s32[8,16]{1,0:T(8,128)} %block_ref.1, s32[128]{0:T(128)} %length_ref.1, s32[16]{0:T(128)} %partner_ref.1, s32[16]{0:T(128)} %moved_ref.1, bf16[4,8,4096]{2,1,0:T(8,128)(2,1)} %step_q_ref.1, bf16[4,8,4,256]{3,2,1,0:T(4,128)(2,1)} %step_kv_ref.1, ...), custom_call_target="tpu_custom_call" | custom-call | tf_op jit(solution)/shard_map/pallas_call | solution.py:507
  77.4 0.7 copy.14
  78.1 1.3 %copy.15 = bf16[256,4096]{1,0:T(8,128)(2,1)} copy(bf16[256,4096]{1,0:T(8,128)(2,1)S(1)} %get-tuple-element.3) | data formatting | bytes 4194304

commit v4 on v3

--- a/solution.py
+++ b/solution.py
@@ -181,14 +181,6 @@
         tp = lax.rem(me_tp + turn % n_tp, n_tp)
         pl.semaphore_signal(barrier, inc=1, device_id=(inst, tp), device_id_type=MESH)
 
-    for t in range(steps):
-        for h in range(heads):
-            step_ref[t * heads + h] = step_q_ref[t, :, h * head : (h + 1) * head].astype(f32)
-    my_slot = moved_ref[me_inst]
-    distance = partner_ref[me_inst] - me_inst
-    move_q_out[...] = step_ref[:, my_slot, :].astype(bf16)
-    move_kv_out[...] = step_kv_ref[:, my_slot].reshape(steps * kv_heads, both)
-
     lanes = n_tp * rows
     mine = target_ref[pl.ds(me_inst, 1), :]
     onehot = (lax.broadcasted_iota(jnp.int32, (n_inst, lanes), 0) == mine).astype(f32)
@@ -204,21 +196,40 @@
     dispatch = both_rows[:, :rows]
     for tp in range(1, n_tp):
         dispatch = jnp.where(me_tp == tp, both_rows[:, tp * rows : (tp + 1) * rows], dispatch)
-    dispatch = dispatch.astype(bf16)
-
-    def pack(tp):
+
+    half = n_inst // 2
+    local_inst = lax.rem(me_inst, half)
+    near_base = me_inst - local_inst
+    far_base = half - near_base
+    is_low = me_inst < half
+    low, high = dispatch[: half * cap], dispatch[half * cap :]
+    far_rows = jnp.where(is_low, high, low).astype(bf16)
+    near_rows = jnp.where(is_low, low, high).astype(bf16)
+
+    def pack(tp, base, chosen):
+        insts = pl.ds(base, half)
         for h in range(kv_heads):
             start = h * group * head
             queries = prompt_q_ref[tp, :, start : start + group * head]
-            packed = jnp.dot(dispatch, queries, preferred_element_type=f32)
-            send_ref[tp, :, :, h * unit : h * unit + group * head] = packed.reshape(
-                n_inst, cap, group * head
+            packed = jnp.dot(chosen, queries, preferred_element_type=f32)
+            send_ref[tp, insts, :, h * unit : h * unit + group * head] = packed.reshape(
+                half, cap, group * head
             ).astype(bf16)
             keyvals = prompt_kv_ref[:, tp * kv_heads + h, :]
-            packed = jnp.dot(dispatch, keyvals, preferred_element_type=f32)
-            send_ref[tp, :, :, h * unit + group * head : (h + 1) * unit] = packed.reshape(
-                n_inst, cap, both
+            packed = jnp.dot(chosen, keyvals, preferred_element_type=f32)
+            send_ref[tp, insts, :, h * unit + group * head : (h + 1) * unit] = packed.reshape(
+                half, cap, both
             ).astype(bf16)
+
+    my_slot = moved_ref[me_inst]
+    distance = partner_ref[me_inst] - me_inst
+
+    def prepare_moves():
+        for t in range(steps):
+            for h in range(heads):
+                step_ref[t * heads + h] = step_q_ref[t, :, h * head : (h + 1) * head].astype(f32)
+        move_q_out[...] = step_ref[:, my_slot, :].astype(bf16)
+        move_kv_out[...] = step_kv_ref[:, my_slot].reshape(steps * kv_heads, both)
 
     def neighbour(bit):
         return me_inst + (1 - 2 * lax.rem(me_inst // (1 << bit), 2)) * (1 << bit)
@@ -248,23 +259,21 @@
             device_id_type=MESH,
         )
 
-    half = n_inst // 2
-    order = []
-    for j in range(half):
-        order.extend([half + j, j])
     for tp in range(n_tp):
         prompt_copies[tp].wait()
-        pack(tp)
+        pack(tp, far_base, far_rows)
         if tp == 0:
             pl.semaphore_wait(barrier, devices - 1)
+        for j in range(half):
+            shipment(far_base + lax.rem(local_inst + j, half), tp, me).start()
+        if tp == 0:
+            prepare_moves()
             for copy in moves:
                 copy.start()
-        for j in order:
-            inst = lax.rem(me_inst + j, n_inst)
-            if j:
-                shipment(inst, tp, me).start()
-            else:
-                pl.when(me_tp != tp)(lambda: shipment(me_inst, tp, me).start())
+        pack(tp, near_base, near_rows)
+        for j in range(1, half):
+            shipment(near_base + lax.rem(local_inst + j, half), tp, me).start()
+        pl.when(me_tp != tp)(lambda: shipment(me_inst, tp, me).start())
     own = pltpu.make_async_copy(send_ref.at[me_tp, me_inst], recv_ref.at[me], self_sem)
     own.start()
 
@@ -356,25 +365,8 @@
     returns = [move(bit, move_o_out, move_o_in, 2) for bit in range(bits)]
     for copy in returns:
         copy.start()
-    for copy in returns:
-        copy.wait()
-    moved_o = move_o_in[0].astype(f32)
-    for bit in range(1, bits):
-        match = (distance == (1 << bit)) | (distance == -(1 << bit))
-        moved_o = jnp.where(match, move_o_in[bit].astype(f32), moved_o)
-    slot_row = lax.broadcasted_iota(jnp.int32, (requests, 1), 0)
-    for t in range(steps):
-        for h in range(heads):
-            row = t * heads + h
-            decode_ref[t, :, h * head : (h + 1) * head] = jnp.where(
-                slot_row == my_slot, moved_o[row : row + 1, :], decoded_ref[row]
-            ).astype(bf16)
 
     size = slots // 2
-    local_inst = lax.rem(me_inst, half)
-    near_base = me_inst - local_inst
-    far_base = half - near_base
-    is_low = me_inst < half
 
     def take(part, column, count):
         first = part * (devices // 2)
@@ -469,6 +461,20 @@
             shipment(me_inst, me_tp, source).wait_recv()
     pl.when(is_low)(loop(upper_all))
     pl.when(jnp.logical_not(is_low))(loop(lower_then_upper))
+
+    for copy in returns:
+        copy.wait()
+    moved_o = move_o_in[0].astype(f32)
+    for bit in range(1, bits):
+        match = (distance == (1 << bit)) | (distance == -(1 << bit))
+        moved_o = jnp.where(match, move_o_in[bit].astype(f32), moved_o)
+    slot_row = lax.broadcasted_iota(jnp.int32, (requests, 1), 0)
+    for t in range(steps):
+        for h in range(heads):
+            row = t * heads + h
+            decode_ref[t, :, h * head : (h + 1) * head] = jnp.where(
+                slot_row == my_slot, moved_o[row : row + 1, :], decoded_ref[row]
+            ).astype(bf16)
 
     for j in range(n_inst):
         for t in range(n_tp):

time: 79.6 us -> 78.8 us (0.990); the launches traced: 79.4 us -> 77.7 us
  Pallas kernels: 76.8 us -> 75 us
    pallas_call x1, Pallas kernels: 76.8 us -> 75 us  [local_fused(): pl.pallas_call(functools.partial(fused_kernel, n_inst, n_tp), out_shape=(...]
where the time goes in v4:
time: 78.8 us; the launch traced here: 77.7 us
  Pallas kernels  75 us (95%)
  local copies, waits for them, and re-layouts  2.02 us (3%)
    pallas_call x1, Pallas kernels, local_fused(): pl.pallas_call(functools.partial(fused_kernel, n_inst, n_tp), out_shape=(...  75 us
    unnamed x2, local copies, waits for them, and re-layouts  2.02 us

profile of v4, /device:TPU:28, one launch (start us, length us, event | category | flops | bytes accessed | tf_op | source)
XLA Modules:
  0.0 77.7 jit_solution(8097736064578443986)
XLA Ops:
  0.6 75.0 %shard_map.113 = (bf16[4,8,4096]{2,1,0:T(8,128)(2,1)S(1)}, bf16[256,4096]{1,0:T(8,128)(2,1)S(1)}) custom-call(s32[8,16]{1,0:T(8,128)} %block_ref.1, s32[128]{0:T(128)} %length_ref.1, s32[16]{0:T(128)} %partner_ref.1, s32[16]{0:T(128)} %moved_ref.1, bf16[4,8,4096]{2,1,0:T(8,128)(2,1)} %step_q_ref.1, bf16[4,8,4,256]{3,2,1,0:T(4,128)(2,1)} %step_kv_ref.1, ...), custom_call_target="tpu_custom_call" | custom-call | tf_op jit(solution)/shard_map/pallas_call | solution.py:513
  75.7 0.7 copy.14
  76.4 1.3 %copy.15 = bf16[256,4096]{1,0:T(8,128)(2,1)} copy(bf16[256,4096]{1,0:T(8,128)(2,1)S(1)} %get-tuple-element.3) | data formatting | bytes 4194304

commit v5 on v4

--- a/solution.py
+++ b/solution.py
@@ -112,16 +112,19 @@
     length_ref,
     partner_ref,
     moved_ref,
-    step_q_ref,
-    step_kv_ref,
+    step_q_hbm,
+    step_kv_hbm,
     cache_hbm,
     prompt_q_hbm,
-    prompt_kv_ref,
+    prompt_kv_hbm,
     target_ref,
     decode_ref,
     prefill_ref,
     cache_ref,
+    step_q_ref,
+    step_kv_ref,
     prompt_q_ref,
+    prompt_kv_ref,
     send_ref,
     recv_ref,
     step_ref,
@@ -138,6 +141,7 @@
     part_ref,
     part_top_ref,
     cache_sem,
+    small_sem,
     prompt_sem,
     self_sem,
     send_sem,
@@ -150,7 +154,7 @@
     me = me_inst * n_tp + me_tp
     devices = n_inst * n_tp
     bits = n_inst.bit_length() - 1
-    steps, requests, width = step_q_ref.shape
+    steps, requests, width = step_q_hbm.shape
     kv_heads, both = step_kv_ref.shape[2:]
     head = both // 2
     heads = width // head
@@ -162,15 +166,29 @@
     unit = group * head + both
     factor = head**-0.5 * math.log2(math.e)
 
+    tps = [lax.rem(me_tp + t, n_tp) for t in range(n_tp)]
     prompt_copies = [
         pltpu.make_async_copy(
-            prompt_q_hbm.at[:, tp * width : (tp + 1) * width],
-            prompt_q_ref.at[tp],
-            prompt_sem.at[tp],
-        )
-        for tp in range(n_tp)
+            prompt_q_hbm.at[:, pl.ds(pl.multiple_of(tps[t] * width, 128), width)],
+            prompt_q_ref.at[t],
+            prompt_sem.at[t],
+        )
+        for t in range(n_tp)
     ]
+    small_copies = [
+        pltpu.make_async_copy(source, target, small_sem.at[i])
+        for i, (source, target) in enumerate(
+            [
+                (prompt_kv_hbm, prompt_kv_ref),
+                (step_q_hbm, step_q_ref),
+                (step_kv_hbm, step_kv_ref),
+            ]
+        )
+    ]
+    small_copies[0].start()
     for copy in prompt_copies:
+        copy.start()
+    for copy in small_copies[1:]:
         copy.start()
     cache_copy = pltpu.make_async_copy(cache_hbm, cache_ref, cache_sem)
     cache_copy.start()
@@ -206,25 +224,31 @@
     far_rows = jnp.where(is_low, high, low).astype(bf16)
     near_rows = jnp.where(is_low, low, high).astype(bf16)
 
-    def pack(tp, base, chosen):
+    def pack(t, base, chosen):
         insts = pl.ds(base, half)
         for h in range(kv_heads):
             start = h * group * head
-            queries = prompt_q_ref[tp, :, start : start + group * head]
+            queries = prompt_q_ref[t, :, start : start + group * head]
             packed = jnp.dot(chosen, queries, preferred_element_type=f32)
-            send_ref[tp, insts, :, h * unit : h * unit + group * head] = packed.reshape(
+            send_ref[tps[t], insts, :, h * unit : h * unit + group * head] = packed.reshape(
                 half, cap, group * head
             ).astype(bf16)
-            keyvals = prompt_kv_ref[:, tp * kv_heads + h, :]
+            keyvals = prompt_kv_ref[:, h, :]
+            for tp in range(1, n_tp):
+                keyvals = jnp.where(
+                    tps[t] == tp, prompt_kv_ref[:, tp * kv_heads + h, :], keyvals
+                )
             packed = jnp.dot(chosen, keyvals, preferred_element_type=f32)
-            send_ref[tp, insts, :, h * unit + group * head : (h + 1) * unit] = packed.reshape(
-                half, cap, both
-            ).astype(bf16)
+            send_ref[tps[t], insts, :, h * unit + group * head : (h + 1) * unit] = (
+                packed.reshape(half, cap, both).astype(bf16)
+            )
 
     my_slot = moved_ref[me_inst]
     distance = partner_ref[me_inst] - me_inst
 
     def prepare_moves():
+        for copy in small_copies[1:]:
+            copy.wait()
         for t in range(steps):
             for h in range(heads):
                 step_ref[t * heads + h] = step_q_ref[t, :, h * head : (h + 1) * head].astype(f32)
@@ -259,21 +283,22 @@
             device_id_type=MESH,
         )
 
-    for tp in range(n_tp):
-        prompt_copies[tp].wait()
-        pack(tp, far_base, far_rows)
-        if tp == 0:
+    small_copies[0].wait()
+    for t in range(n_tp):
+        prompt_copies[t].wait()
+        pack(t, far_base, far_rows)
+        if t == 0:
             pl.semaphore_wait(barrier, devices - 1)
         for j in range(half):
-            shipment(far_base + lax.rem(local_inst + j, half), tp, me).start()
-        if tp == 0:
+            shipment(far_base + lax.rem(local_inst + j, half), tps[t], me).start()
+        if t == 0:
             prepare_moves()
             for copy in moves:
                 copy.start()
-        pack(tp, near_base, near_rows)
-        for j in range(1, half):
-            shipment(near_base + lax.rem(local_inst + j, half), tp, me).start()
-        pl.when(me_tp != tp)(lambda: shipment(me_inst, tp, me).start())
+        pack(t, near_base, near_rows)
+        for j in range(half):
+            if j or t:
+                shipment(near_base + lax.rem(local_inst + j, half), tps[t], me).start()
     own = pltpu.make_async_copy(send_ref.at[me_tp, me_inst], recv_ref.at[me], self_sem)
     own.start()
 
@@ -517,11 +542,14 @@
             pltpu.VMEM((slots, width), bf16),
         ),
         in_specs=[smem] * 4
-        + [vmem, vmem, hbm, hbm, vmem, vmem],
+        + [hbm] * 5 + [vmem],
         out_specs=(vmem, vmem),
         scratch_shapes=[
             pltpu.VMEM(cache_pages.shape, bf16),
+            pltpu.VMEM(step_queries.shape, bf16),
+            pltpu.VMEM(step_keyvals.shape, bf16),
             pltpu.VMEM((n_tp, prompt_queries.shape[0], width), bf16),
+            pltpu.VMEM(prompt_keyvals.shape, bf16),
             pltpu.VMEM((n_tp, n_inst, cap, columns), bf16),
             pltpu.VMEM((devices, cap, columns), bf16),
             pltpu.VMEM((steps * heads, requests, head), f32),
@@ -538,6 +566,7 @@
             pltpu.VMEM((kv_heads, heads // kv_heads * slots // 2, both), f32),
             pltpu.VMEM((kv_heads, heads // kv_heads * slots // 2, head), f32),
             pltpu.SemaphoreType.DMA,
+            pltpu.SemaphoreType.DMA((3,)),
             pltpu.SemaphoreType.DMA((n_tp,)),
             pltpu.SemaphoreType.DMA,
             pltpu.SemaphoreType.DMA((devices,)),

time: 78.8 us -> 75.3 us (0.956)
  Pallas kernels: 75 us -> 71.3 us
    pallas_call x1, Pallas kernels: 75 us -> 71.3 us  [local_fused(): pl.pallas_call(functools.partial(fused_kernel, n_inst, n_tp), out_shape=(...]
where the time goes in v5:
time: 75.3 us; the launch traced here: 73.9 us
  Pallas kernels  71.3 us (95%)
  local copies, waits for them, and re-layouts  2.02 us (3%)
    pallas_call x1, Pallas kernels, local_fused(): pl.pallas_call(functools.partial(fused_kernel, n_inst, n_tp), out_shape=(...  71.3 us
    unnamed x2, local copies, waits for them, and re-layouts  2.02 us

profile of v5, /device:TPU:28, one launch (start us, length us, event | category | flops | bytes accessed | tf_op | source)
XLA Modules:
  0.0 73.9 jit_solution(9717359380004679726)
XLA Ops:
  0.6 71.3 %shard_map.113 = (bf16[4,8,4096]{2,1,0:T(8,128)(2,1)S(1)}, bf16[256,4096]{1,0:T(8,128)(2,1)S(1)}) custom-call(s32[8,16]{1,0:T(8,128)} %block_ref.1, s32[128]{0:T(128)} %length_ref.1, s32[16]{0:T(128)} %partner_ref.1, s32[16]{0:T(128)} %moved_ref.1, bf16[4,8,4096]{2,1,0:T(8,128)(2,1)} %step_q_hbm.1, bf16[4,8,4,256]{3,2,1,0:T(4,128)(2,1)} %step_kv_hbm.1, ...), custom_call_target="tpu_custom_call" | custom-call | tf_op jit(solution)/shard_map/pallas_call | solution.py:538
  71.9 0.7 copy.14
  72.6 1.3 %copy.15 = bf16[256,4096]{1,0:T(8,128)(2,1)} copy(bf16[256,4096]{1,0:T(8,128)(2,1)S(1)} %get-tuple-element.3) | data formatting | bytes 4194304

commit v6 on v5

--- a/solution.py
+++ b/solution.py
@@ -283,22 +283,32 @@
             device_id_type=MESH,
         )
 
+    def send(base, t, j):
+        if base is far_base or j or t:
+            shipment(base + lax.rem(local_inst + j, half), tps[t], me).start()
+
     small_copies[0].wait()
+    far, near = [], []
     for t in range(n_tp):
         prompt_copies[t].wait()
         pack(t, far_base, far_rows)
+        far.extend((t, j) for j in range(half))
         if t == 0:
             pl.semaphore_wait(barrier, devices - 1)
-        for j in range(half):
-            shipment(far_base + lax.rem(local_inst + j, half), tps[t], me).start()
-        if t == 0:
+            send(far_base, *far.pop(0))
+            send(far_base, *far.pop(0))
             prepare_moves()
             for copy in moves:
                 copy.start()
         pack(t, near_base, near_rows)
-        for j in range(half):
-            if j or t:
-                shipment(near_base + lax.rem(local_inst + j, half), tps[t], me).start()
+        near.extend((t, j) for j in range(half))
+        while far:
+            for _ in range(-(-len(near) // len(far)) if t == n_tp - 1 else 1):
+                if near:
+                    send(near_base, *near.pop(0))
+            send(far_base, *far.pop(0))
+    for entry in near:
+        send(near_base, *entry)
     own = pltpu.make_async_copy(send_ref.at[me_tp, me_inst], recv_ref.at[me], self_sem)
     own.start()
 

time: 75.3 us -> 74.7 us (level)
  no operation moved by 1% of the time
where the time goes in v6:
time: 74.7 us; the launch traced here: 73.5 us
  Pallas kernels  70.9 us (95%)
  local copies, waits for them, and re-layouts  2.02 us (3%)
    pallas_call x1, Pallas kernels, local_fused(): pl.pallas_call(functools.partial(fused_kernel, n_inst, n_tp), out_shape=(...  70.9 us
    unnamed x2, local copies, waits for them, and re-layouts  2.02 us

profile of v6, /device:TPU:28, one launch (start us, length us, event | category | flops | bytes accessed | tf_op | source)
XLA Modules:
  0.0 73.5 jit_solution(1049214967084856634)
XLA Ops:
  0.6 70.9 %shard_map.113 = (bf16[4,8,4096]{2,1,0:T(8,128)(2,1)S(1)}, bf16[256,4096]{1,0:T(8,128)(2,1)S(1)}) custom-call(s32[8,16]{1,0:T(8,128)} %block_ref.1, s32[128]{0:T(128)} %length_ref.1, s32[16]{0:T(128)} %partner_ref.1, s32[16]{0:T(128)} %moved_ref.1, bf16[4,8,4096]{2,1,0:T(8,128)(2,1)} %step_q_hbm.1, bf16[4,8,4,256]{3,2,1,0:T(4,128)(2,1)} %step_kv_hbm.1, ...), custom_call_target="tpu_custom_call" | custom-call | tf_op jit(solution)/shard_map/pallas_call | solution.py:548
  71.5 0.7 copy.14
  72.2 1.3 %copy.15 = bf16[256,4096]{1,0:T(8,128)(2,1)} copy(bf16[256,4096]{1,0:T(8,128)(2,1)S(1)} %get-tuple-element.3) | data formatting | bytes 4194304
